TPU v7x, 32 devices: a whole 2x2x4 slice. The times are simulated.
32 devices in a mesh: dp: 8 (over y, x, core), fsdp: 4 (over z).
Axes of the slice: x: 2, y: 2, z: 4, core: 2. Of those that a mesh axis runs over, the one named last changes fastest.
Arguments:
- grad_partials: bfloat16 [8, 4, 2, 16, 5120], P('dp', 'fsdp'), may hold values from -5 to 5
- momentum: float32 [8, 2, 16, 5120], P('dp', None, 'fsdp'), may hold values from -6 to 6
- params: float32 [2, 16, 5120], P(None, 'fsdp'), may hold values from -6 to 6
- kept: int32 [8], replicated, may hold values from 0 to 63, as said below
Outputs:
- new_params: float32 [2, 16, 5120], P(None, 'fsdp')
- new_momentum: float32 [8, 2, 16, 5120], P('dp', None, 'fsdp')
Inputs may be any that keep to these rules, and one draw needn't show every extreme that they name: `kept`: 8 distinct coefficient indices.
All inputs are finite; a program needn't handle non-finite values.
Results may differ from a plain program's by a relative error of at most 0.0003.
Values sent between devices are 32-bit elements; how exact they have to be, the bound alone decides.
A program may use at most 64 MiB of HBM per device.

v0:
```python
import jax
import jax.numpy as jnp
from jax import lax
from jax.sharding import PartitionSpec as P

SPAN = 64
KEEP = 8
ROW_VALS = 5120


def dct_table():
    k = lax.broadcasted_iota(jnp.float32, (SPAN, SPAN), 0)
    n = lax.broadcasted_iota(jnp.float32, (SPAN, SPAN), 1)
    scale = jnp.where(k == 0, jnp.sqrt(1.0 / SPAN), jnp.sqrt(2.0 / SPAN))
    return scale * jnp.cos(jnp.pi * (2.0 * n + 1.0) * k / (2.0 * SPAN))


def shards(grad_partials, momentum, params, kept):
    blocks = ROW_VALS // SPAN
    table = dct_table()
    onehot = (kept[:, None] == jnp.arange(SPAN, dtype=jnp.int32)[None, :]).astype(jnp.float32)
    picked = jnp.dot(onehot, table, precision=lax.Precision.HIGHEST)
    terms = grad_partials[0, 0].astype(jnp.float32)
    grad = lax.psum_scatter(terms, "fsdp", scatter_dimension=1, tiled=True)
    moment = 0.9 * momentum[0] + grad
    layer_count = moment.shape[0]
    row_count = moment.shape[1]
    spans = moment.reshape(layer_count, row_count, blocks, SPAN)
    spectra = jnp.einsum("lrcn,kn->lrck", spans, table, precision=lax.Precision.HIGHEST)
    coeffs = jnp.take(spectra, kept, axis=3)
    local = jnp.einsum("lrcj,jn->lrcn", coeffs, picked, precision=lax.Precision.HIGHEST)
    new_momentum = (moment - local.reshape(moment.shape))[None]
    flat_coeffs = coeffs.reshape(layer_count, row_count, blocks * KEEP)
    replicas = lax.axis_size("dp")
    total = jnp.sum(lax.all_gather(flat_coeffs[None], "dp", axis=0, tiled=True), axis=0)
    shared = (total / replicas).reshape(layer_count, row_count, blocks, KEEP)
    update = jnp.einsum("lrcj,jn->lrcn", shared, picked, precision=lax.Precision.HIGHEST)
    new_params = params - update.reshape(params.shape)
    return (new_params, new_momentum)


def solution(mesh):
    placed = (
        P("dp", "fsdp", None, None, None),
        P("dp", None, "fsdp", None),
        P(None, "fsdp", None),
        P(),
    )
    return jax.shard_map(
        shards,
        mesh=mesh,
        in_specs=placed,
        out_specs=(P(None, "fsdp", None), P("dp", None, "fsdp", None)),
        check_vma=False,
    )
```

profile of v0, /device:TPU:0, one launch (start us, length us, event | category | flops | bytes accessed | tf_op | source)
XLA Modules:
  0.0 76.5 jit_solution(16315492341597944272)
XLA Ops:
  7.2 0.0 all-reduce.3.cloned.1.call-start
  7.2 1.9 %bitcast_convert_fusion = f32[2,16,5120]{2,1,0:T(8,128)} fusion(bf16[1,1,2,16,5120]{4,3,2,1,0:T(8,128)(2,1)} %param.4), kind=kLoop, calls=%fused_computation.2 | loop fusion | flops 163840 | bytes 983040 | tf_op jit(solution)/shard_map/convert_element_type | solution.py:23
  9.1 0.0 copy-start.2
  9.1 0.0 copy-start.3
  9.1 0.0 all-reduce.3.cloned.1.call-update
  9.1 0.0 copy-start
  9.1 0.6 copy-done.2
  9.8 0.1 broadcast_in_dim.34
  9.9 0.0 copy-done.3
  9.9 0.6 dynamic-slice
  11.2 0.3 convolution_bitcast_fusion
  11.5 42.1 %all-reduce.3.cloned.1.call-done = f32[2,16,5120]{2,1,0:T(8,128)} async-done(((f32[2,16,5120]{2,1,0:T(8,128)}), f32[2,16,5120]{2,1,0:T(8,128)}) %all-reduce.3.cloned.1.call-update) | async-done | bytes 655376
  53.6 0.0 copy-done
  53.6 1.0 %dynamic-slice_add_fusion = f32[2,4,5120]{2,1,0:T(4,128)S(1)} fusion(f32[2,16,5120]{2,1,0:T(8,128)} %all-reduce.3.cloned.1.call-done, u32[]{:T(128)S(6)} %multiply.7, f32[1,2,4,5120]{3,2,1,0:T(4,128)S(1)} %copy-done), kind=kLoop, calls=%fused_computation.3 | loop fusion | flops 81920 | bytes 491524 | tf_op jit(solution)/shard_map/add | solution.py:25
  54.6 0.2 reshape.38
  54.8 1.0 %fusion = f32[2,4,80,64]{2,3,1,0:T(8,128)S(1)} fusion(f32[2,4,80,64]{3,2,1,0:T(8,128)S(1)} %reshape.38, f32[64]{0:T(128)S(1)} %get-tuple-element.3, f32[64]{0:T(128)S(1)} %multiply_add_fusion, f32[64]{0:T(128)S(1)} %get-tuple-element.2), kind=kOutput, calls=%fused_computation.5 | convolution fusion | flops 31469568 | bytes 328448 | tf_op jit(solution)/shard_map/lrcn,kn->lrck/dot_general | solution.py:29
  55.8 0.2 copy.15
  56.0 0.6 gather_fusion
  56.6 0.1 broadcast_select_fusion
  56.7 0.1 copy.16
  56.8 0.2 gather.7
  57.1 9.2 %all_gather.3 = f32[8,2,4,640]{3,2,1,0:T(4,128)S(1)} all-gather(f32[1,2,4,640]{3,2,1,0:T(4,128)S(1)} %broadcast_select_fusion.1), channel_id=1, replica_groups=mesh['dp'=8,'fsdp'=4] {'dp'}, dimensions={0}, use_global_device_ids=true | all-gather | bytes 184320 | tf_op jit(solution)/shard_map/all_gather | solution.py:35
  66.3 0.2 div.20
  66.5 0.4 fusion.15
  66.9 0.2 reshape.39
  67.1 0.7 fusion.2
  67.8 0.2 reshape.40
  68.0 0.0 copy-start.1
  68.0 0.7 subtract_bitcast_fusion
  68.7 0.2 copy-done.1
  68.9 0.7 sub.6
  (9 shorter events, 0.1 us)
Async XLA Ops:
  7.2 46.4 %all-reduce.3.cloned.1.call-start = ((), (), s32[]{:S(2)}) async-start(), calls=%async_computation | async-start | bytes 1310720
  9.1 0.7 copy-start.2
  9.1 0.8 %copy-start.3 = (u32[32]{0:T(128)S(1)}, u32[32]{0:T(128)}, u32[]{:S(2)}) copy-start(u32[32]{0:T(128)} %constant.40) | copy-start | bytes 388
  9.1 44.5 %copy-start = (f32[1,2,4,5120]{3,2,1,0:T(4,128)S(1)}, f32[1,2,4,5120]{3,2,1,0:T(4,128)}, u32[]{:S(2)}) copy-start(f32[1,2,4,5120]{3,2,1,0:T(4,128)} %param.5) | copy-start | bytes 491524
  68.0 0.9 %copy-start.1 = (f32[2,4,5120]{2,1,0:T(4,128)S(1)}, f32[2,4,5120]{2,1,0:T(4,128)}, u32[]{:S(2)}) copy-start(f32[2,4,5120]{2,1,0:T(4,128)} %param.6) | copy-start | bytes 491524
Sparse Core Ops, SparseCore 0:
  10.4 43.1 all-reduce.2
where the time goes:
time: 76.8 us; the launch traced here: 76.5 us
  waiting for transfers between devices  42.1 us (55%)
  between operations  14.8 us (19%)
  blocking collectives  9.23 us (12%)
  other arithmetic  4.48 us (6%)
  local copies, waits for them, and re-layouts  3.36 us (4%)
  matrix products  2.45 us (3%)
    unnamed x2, waiting for transfers between devices  42.1 us
    all_gather x1, blocking collectives, shards(): lax.all_gather(flat_coeffs[None], 'dp', axis=0, tiled=True)  9.23 us
    convert_element_type x1, other arithmetic, shards(): terms = grad_partials[0, 0].astype(jnp.float32)  1.87 us
  transfers between devices with their start and end apart: 1, of which 1 were waited for; matrix products, arithmetic and copies ran while one was open for 1% of the time, Pallas kernels for 0%

commit v1 on v0

v1 whole, which is shorter than its diff:
```python
import functools
import math

import jax
import jax.numpy as jnp
from jax import lax
from jax.experimental import pallas as pl
from jax.experimental.pallas import tpu as pltpu
from jax.sharding import PartitionSpec as P

SPAN = 64
KEEP = 8
PIECE = 1024
GROUP = 256
LAG = 2
F32 = jnp.float32
BF16 = jnp.bfloat16


def cosine_rows(k, n):
    turn = ((2 * n + 1) * k) & (4 * SPAN - 1)
    turn = jnp.minimum(turn, 4 * SPAN - turn)
    scale = jnp.where(k == 0, math.sqrt(1.0 / SPAN), math.sqrt(2.0 / SPAN)).astype(F32)
    return scale * jnp.cos(turn.astype(F32) * (math.pi / (2 * SPAN)))


def halves(x):
    high = x.astype(BF16)
    return high, (x - high.astype(F32)).astype(BF16)


def dot(a, b):
    return jnp.dot(a, b, preferred_element_type=F32)


def kernel(
    n_dp, n_fsdp, batches,
    grad_hbm, mom_hbm, par_hbm, kept_ref, new_par_hbm, new_mom_hbm,
    grad, mom, par, mine, inbox, coeffs, w_coef, w_proj, w_back, new_par, new_mom,
    load_sem, store_sem, send_sem, recv_sem, dp_send, dp_recv,
):
    layers, rows, cols = grad.shape
    own = rows // n_fsdp
    pieces = cols // PIECE
    dp, me = lax.axis_index("dp"), lax.axis_index("fsdp")

    loads = [
        pltpu.make_async_copy(grad_hbm.at[0, 0], grad, load_sem.at[0]),
        pltpu.make_async_copy(mom_hbm.at[0], mom, load_sem.at[1]),
        pltpu.make_async_copy(par_hbm, par, load_sem.at[2]),
    ]
    for load in loads:
        load.start()

    barrier = pltpu.get_barrier_semaphore()
    for i in range(1, n_dp):
        pl.semaphore_signal(
            barrier, inc=1, device_id={"dp": lax.rem(dp + i, n_dp)}, device_id_type=pl.DeviceIdType.MESH
        )

    near = me // (n_fsdp // 2)
    far = 1 - near
    near_pos = near * (n_fsdp - 1 - me) + far * me
    far_pos = n_fsdp - 1 - near_pos
    near_next, far_next = me + 1 - 2 * near, me + 1 - 2 * far
    pl.semaphore_signal(barrier, inc=1, device_id={"fsdp": near_next}, device_id_type=pl.DeviceIdType.MESH)

    @pl.when(near_pos > 0)
    def _():
        pl.semaphore_signal(barrier, inc=1, device_id={"fsdp": far_next}, device_id_type=pl.DeviceIdType.MESH)

    loads[0].wait()
    for layer in range(layers):
        for p in range(pieces):
            at = pl.ds(p * PIECE, PIECE)
            x = grad[layer, :, at].astype(F32)
            for d in range(n_fsdp):
                mine[d, layer * own:(layer + 1) * own, at] = x[d * own:(d + 1) * own]

    pl.semaphore_wait(barrier, n_dp + (near_pos > 0).astype(jnp.int32))

    def forward(flow, q, p):
        at = pl.ds(p * PIECE, PIECE)
        d = flow * (n_fsdp - 1 - q) + (1 - flow) * q
        return pltpu.make_async_remote_copy(
            src_ref=mine.at[d, :, at], dst_ref=inbox.at[flow, d, :, at],
            send_sem=send_sem.at[flow, q, p], recv_sem=recv_sem.at[flow, q, p],
            device_id={"fsdp": me + 1 - 2 * flow}, device_id_type=pl.DeviceIdType.MESH,
        )

    def add(flow, q, p):
        at = pl.ds(p * PIECE, PIECE)
        d = flow * (n_fsdp - 1 - q) + (1 - flow) * q
        forward(flow, q, p).wait_recv()
        mine[d, :, at] += inbox[flow, d, :, at]

    near_list = [(q, p) for q in range(n_fsdp - 1, 0, -1) for p in range(pieces)]
    far_list = [(q, p) for q in range(n_fsdp - 1, n_fsdp // 2, -1) for p in range(pieces)]

    @pl.when(near_pos == 0)
    def _():
        for q, p in near_list:
            forward(near, q, p).start()

    def by_index(shape, dim):
        j = lax.broadcasted_iota(jnp.int32, shape, dim) % KEEP
        k = jnp.zeros(shape, jnp.int32)
        for i in range(KEEP):
            k = jnp.where(j == i, kept_ref[i], k)
        return k

    lanes = 128
    row = cosine_rows(by_index((KEEP, lanes), 0), lax.broadcasted_iota(jnp.int32, (KEEP, lanes), 1) % SPAN)
    column = cosine_rows(by_index((SPAN, lanes), 1), lax.broadcasted_iota(jnp.int32, (SPAN, lanes), 0))
    lane_block = lax.broadcasted_iota(jnp.int32, (SPAN, lanes), 1) // KEEP
    coef = jnp.concatenate([jnp.where(lane_block == b, column, 0.0) for b in range(GROUP // SPAN)], axis=0)
    wide = jnp.concatenate([row] * (PIECE // lanes), axis=1)
    wide_block = lax.broadcasted_iota(jnp.int32, (KEEP, PIECE), 1) // SPAN
    back = jnp.concatenate([jnp.where(wide_block == b, wide, 0.0) for b in range(PIECE // SPAN)], axis=0)
    high, low = halves(coef)
    w_coef[:, :lanes] = high
    w_coef[:, lanes:] = low
    high, low = halves(back)
    w_back[:lanes] = high
    w_back[lanes:] = low
    proj = jnp.dot(coef, back[:, :GROUP], precision=lax.Precision.HIGHEST, preferred_element_type=F32)
    high, low = halves(proj)
    w_proj[:, :GROUP] = high
    w_proj[:, GROUP:] = low

    def near_step(q, p):
        @pl.when((near_pos > 0) & (near_pos < q))
        def _():
            add(near, q, p)
            forward(near, q, p).start()

    def far_step(q, p):
        @pl.when(far_pos < q)
        def _():
            add(far, q, p)
            forward(far, q, p).start()

    for i in range(len(near_list)):
        if near_list[i][0] > 1:
            near_step(*near_list[i])
        if 0 <= i - LAG < len(far_list):
            far_step(*far_list[i - LAG])

    def dp_copy(i, batch):
        at = pl.ds(batch[0], batch[1] - batch[0])
        b = batches.index(batch)
        return pltpu.make_async_remote_copy(
            src_ref=coeffs.at[dp, at], dst_ref=coeffs.at[dp, at],
            send_sem=dp_send.at[i, b], recv_sem=dp_recv.at[i, b],
            device_id={"dp": lax.rem(dp + i, n_dp)}, device_id_type=pl.DeviceIdType.MESH,
        )

    def dp_arrival(i, batch):
        at = pl.ds(batch[0], batch[1] - batch[0])
        b = batches.index(batch)
        source = lax.rem(dp + n_dp - i, n_dp)
        return pltpu.make_async_remote_copy(
            src_ref=coeffs.at[source, at], dst_ref=coeffs.at[source, at],
            send_sem=dp_send.at[i, b], recv_sem=dp_recv.at[i, b],
            device_id={"dp": lax.rem(dp + i, n_dp)}, device_id_type=pl.DeviceIdType.MESH,
        )

    loads[1].wait()
    parts = PIECE // GROUP
    for batch in batches:
        kept_parts = []
        for p in range(*batch):
            at = pl.ds(p * PIECE, PIECE)
            add(far, far_pos, p)

            @pl.when(near_pos > 0)
            def _():
                add(near, near_pos, p)

            old = jnp.concatenate([mom[layer, :, at] for layer in range(layers)], axis=0)
            moment = 0.9 * old + mine[me, :, at]
            height = moment.shape[0]
            tall = jnp.concatenate([moment[:, q * GROUP:(q + 1) * GROUP] for q in range(parts)], axis=0)
            both = jnp.concatenate(halves(tall), axis=0)
            out = dot(both, w_coef[...])
            out = out[:parts * height] + out[parts * height:]
            out = out[:, :lanes] + out[:, lanes:]
            packed = out[:height]
            for q in range(1, parts):
                packed += pltpu.roll(out[q * height:(q + 1) * height], q * (lanes // parts), 1)
            coeffs[dp, p] = packed
            kept_parts.append((p, tall, both))
        for i in range(1, n_dp):
            dp_copy(i, batch).start()
        for p, tall, both in kept_parts:
            half = tall.shape[0]
            out = dot(both, w_proj[...])
            local = out[:half, :GROUP] + (out[half:, :GROUP] + out[:half, GROUP:])
            rest = tall - local
            height = half // parts
            for q in range(parts):
                at = pl.ds(p * PIECE + q * GROUP, GROUP)
                for layer in range(layers):
                    new_mom[layer, :, at] = rest[q * height + layer * own:q * height + (layer + 1) * own]
    store_mom = pltpu.make_async_copy(new_mom, new_mom_hbm.at[0], store_sem.at[0])
    store_mom.start()

    loads[2].wait()
    for batch in batches:
        for i in range(1, n_dp):
            dp_arrival(i, batch).wait_recv()
        for p in range(*batch):
            at = pl.ds(p * PIECE, PIECE)
            total = coeffs[0, p]
            for r in range(1, n_dp):
                total += coeffs[r, p]
            high, low = halves(total * (1.0 / n_dp) if n_dp & (n_dp - 1) == 0 else total / n_dp)
            height = high.shape[0]
            left = jnp.concatenate([high, low], axis=0)
            right = jnp.concatenate([high, jnp.zeros_like(low)], axis=0)
            out = dot(jnp.concatenate([left, right], axis=1), w_back[...])
            update = out[:height] + out[height:]
            for layer in range(layers):
                new_par[layer, :, at] = par[layer, :, at] - update[layer * own:(layer + 1) * own]
    store_par = pltpu.make_async_copy(new_par, new_par_hbm, store_sem.at[1])
    store_par.start()

    for q, p in near_list:
        @pl.when(near_pos < q)
        def _():
            forward(near, q, p).wait_send()

    for q, p in far_list:
        @pl.when(far_pos < q)
        def _():
            forward(far, q, p).wait_send()

    for batch in batches:
        for i in range(1, n_dp):
            dp_copy(i, batch).wait_send()
    store_mom.wait()
    store_par.wait()


def shards(n_dp, n_fsdp, grad_partials, momentum, params, kept):
    _, _, layers, rows, cols = grad_partials.shape
    own = rows // n_fsdp
    pieces = cols // PIECE
    batches = ((0, pieces // 2), (pieces // 2, pieces - 1), (pieces - 1, pieces))
    held = (layers, own, cols)
    chunk = (n_fsdp, layers * own, cols)
    anywhere = pl.BlockSpec(memory_space=pl.ANY)
    sem = pltpu.SemaphoreType.DMA
    return pl.pallas_call(
        functools.partial(kernel, n_dp, n_fsdp, batches),
        out_shape=(
            jax.ShapeDtypeStruct(params.shape, F32),
            jax.ShapeDtypeStruct(momentum.shape, F32),
        ),
        in_specs=[anywhere, anywhere, anywhere, pl.BlockSpec(memory_space=pltpu.SMEM)],
        out_specs=(anywhere, anywhere),
        scratch_shapes=[
            pltpu.VMEM((layers, rows, cols), BF16),
            pltpu.VMEM(held, F32),
            pltpu.VMEM(held, F32),
            pltpu.VMEM(chunk, F32),
            pltpu.VMEM((2,) + chunk, F32),
            pltpu.VMEM((n_dp, pieces, layers * own, 128), F32),
            pltpu.VMEM((GROUP, 256), BF16),
            pltpu.VMEM((GROUP, 2 * GROUP), BF16),
            pltpu.VMEM((256, PIECE), BF16),
            pltpu.VMEM(held, F32),
            pltpu.VMEM(held, F32),
            sem((3,)),
            sem((2,)),
            sem((2, n_fsdp, pieces)),
            sem((2, n_fsdp, pieces)),
            sem((n_dp, len(batches))),
            sem((n_dp, len(batches))),
        ],
        compiler_params=pltpu.CompilerParams(
            collective_id=0, has_side_effects=True, vmem_limit_bytes=60 * 1024 * 1024
        ),
    )(grad_partials, momentum, params, kept)


def solution(mesh):
    placed = (
        P("dp", "fsdp", None, None, None),
        P("dp", None, "fsdp", None),
        P(None, "fsdp", None),
        P(),
    )
    return jax.shard_map(
        functools.partial(shards, mesh.shape["dp"], mesh.shape["fsdp"]),
        mesh=mesh,
        in_specs=placed,
        out_specs=(P(None, "fsdp", None), P("dp", None, "fsdp", None)),
        check_vma=False,
    )
```

time: 76.8 us -> 26.6 us (0.35)
  waiting for transfers between devices: 42.1 us -> 0 us
  Pallas kernels: 0 us -> 23.3 us
  between operations: 14.8 us -> 0.65 us
  blocking collectives: 9.23 us -> 0 us
  other arithmetic: 4.48 us -> 0 us
  matrix products: 2.45 us -> 0 us
  local copies, waits for them, and re-layouts: 3.36 us -> 2.3 us
    unnamed x2 -> x0, waiting for transfers between devices: 42.1 us -> none
    pallas_call x0 -> x1, Pallas kernels: none -> 23.3 us  [shards(): pl.pallas_call(functools.partial(kernel, n_dp, n_fsdp, batches), out_shap...]
    all_gather x1 -> x0, blocking collectives: 9.23 us -> none  [shards(): lax.all_gather(flat_coeffs[None], 'dp', axis=0, tiled=True)]
    dot_general x4 -> x0, matrix products: 2.45 us -> none  [the longest x1 1.04 us: shards(): jnp.einsum('lrcn,kn->lrck', spans, table, precision=lax.Precision.HIGHEST)]
    convert_element_type x1 -> x0, other arithmetic: 1.87 us -> none  [shards(): terms = grad_partials[0, 0].astype(jnp.float32)]
    add x2 -> x0, other arithmetic: 1.04 us -> none  [the longest x1 1.03 us: shards(): moment = 0.9 * momentum[0] + grad]
    gather x3 -> x0, local copies, waits for them, and re-layouts: 0.93 us -> none  [shards(): coeffs = jnp.take(spectra, kept, axis=3)]
    unnamed x9 -> x4, local copies, waits for them, and re-layouts: 1.42 us -> 2.3 us
  transfers between devices with their start and end apart: 1 -> 0, of which waited for: 1 -> 0; matrix products, arithmetic and copies ran while one was open for 1% -> 0% of each run, Pallas kernels for 0% -> 0%
where the time goes in v1:
time: 26.6 us; the launch traced here: 26.2 us
  Pallas kernels  23.3 us (88%)
  local copies, waits for them, and re-layouts  2.3 us (9%)
  between operations  0.65 us (2%)
    pallas_call x1, Pallas kernels, shards(): pl.pallas_call(functools.partial(kernel, n_dp, n_fsdp, batches), out_shap...  23.3 us
    unnamed x4, local copies, waits for them, and re-layouts  2.3 us

profile of v1, /device:TPU:0, one launch (start us, length us, event | category | flops | bytes accessed | tf_op | source)
XLA Modules:
  0.0 26.2 jit_solution(9599882162220987950)
XLA Ops:
  0.6 23.3 %shard_map.59 = (f32[2,4,5120]{2,1,0:T(4,128)}, f32[1,2,4,5120]{3,2,1,0:T(4,128)}) custom-call(bf16[1,1,2,16,5120]{4,3,2,1,0:T(8,128)(2,1)} %grad_hbm.1, f32[1,2,4,5120]{3,2,1,0:T(4,128)} %mom_hbm.1, f32[2,4,5120]{2,1,0:T(4,128)} %par_hbm.1, s32[8]{0:T(128)} %kept_ref.1), custom_call_target="tpu_custom_call" | custom-call | tf_op jit(solution)/shard_map/pallas_call | solution.py:254
  23.9 0.0 copy-start
  23.9 1.6 %copy.8 = f32[2,4,5120]{2,1,0:T(4,128)} copy(f32[2,4,5120]{2,1,0:T(4,128)} %get-tuple-element.4) | data formatting | bytes 327680
  25.6 0.0 copy-done
  25.6 0.7 %copy.9 = f32[1,2,4,5120]{3,2,1,0:T(4,128)} copy(f32[1,2,4,5120]{3,2,1,0:T(4,128)S(1)} %copy-done) | data formatting | bytes 327680
Async XLA Ops:
  23.9 1.6 %copy-start = (f32[1,2,4,5120]{3,2,1,0:T(4,128)S(1)}, f32[1,2,4,5120]{3,2,1,0:T(4,128)}, u32[]{:S(2)}) copy-start(f32[1,2,4,5120]{3,2,1,0:T(4,128)} %get-tuple-element.5) | copy-start | bytes 491524

commit v2 on v1

--- a/solution.py
+++ b/solution.py
@@ -35,9 +35,9 @@
 
 def kernel(
     n_dp, n_fsdp, batches,
-    grad_hbm, mom_hbm, par_hbm, kept_ref, new_par_hbm, new_mom_hbm,
-    grad, mom, par, mine, inbox, coeffs, w_coef, w_proj, w_back, new_par, new_mom,
-    load_sem, store_sem, send_sem, recv_sem, dp_send, dp_recv,
+    grad_hbm, mom_hbm, par_hbm, kept_hbm, new_par, new_mom,
+    kept_ref, grad, mom, par, mine, inbox, coeffs, w_coef, w_proj, w_back,
+    load_sem, send_sem, recv_sem, dp_send, dp_recv,
 ):
     layers, rows, cols = grad.shape
     own = rows // n_fsdp
@@ -48,6 +48,7 @@
         pltpu.make_async_copy(grad_hbm.at[0, 0], grad, load_sem.at[0]),
         pltpu.make_async_copy(mom_hbm.at[0], mom, load_sem.at[1]),
         pltpu.make_async_copy(par_hbm, par, load_sem.at[2]),
+        pltpu.make_async_copy(kept_hbm, kept_ref, load_sem.at[3]),
     ]
     for load in loads:
         load.start()
@@ -101,6 +102,8 @@
     def _():
         for q, p in near_list:
             forward(near, q, p).start()
+
+    loads[3].wait()
 
     def by_index(shape, dim):
         j = lax.broadcasted_iota(jnp.int32, shape, dim) % KEEP
@@ -202,8 +205,6 @@
                 at = pl.ds(p * PIECE + q * GROUP, GROUP)
                 for layer in range(layers):
                     new_mom[layer, :, at] = rest[q * height + layer * own:q * height + (layer + 1) * own]
-    store_mom = pltpu.make_async_copy(new_mom, new_mom_hbm.at[0], store_sem.at[0])
-    store_mom.start()
 
     loads[2].wait()
     for batch in batches:
@@ -222,8 +223,6 @@
             update = out[:height] + out[height:]
             for layer in range(layers):
                 new_par[layer, :, at] = par[layer, :, at] - update[layer * own:(layer + 1) * own]
-    store_par = pltpu.make_async_copy(new_par, new_par_hbm, store_sem.at[1])
-    store_par.start()
 
     for q, p in near_list:
         @pl.when(near_pos < q)
@@ -238,8 +237,17 @@
     for batch in batches:
         for i in range(1, n_dp):
             dp_copy(i, batch).wait_send()
-    store_mom.wait()
-    store_par.wait()
+
+
+def store(new_par, new_mom, new_par_hbm, new_mom_hbm, sem):
+    copies = [
+        pltpu.make_async_copy(new_par, new_par_hbm, sem.at[0]),
+        pltpu.make_async_copy(new_mom, new_mom_hbm.at[0], sem.at[1]),
+    ]
+    for copy in copies:
+        copy.start()
+    for copy in copies:
+        copy.wait()
 
 
 def shards(n_dp, n_fsdp, grad_partials, momentum, params, kept):
@@ -250,16 +258,16 @@
     held = (layers, own, cols)
     chunk = (n_fsdp, layers * own, cols)
     anywhere = pl.BlockSpec(memory_space=pl.ANY)
+    vmem = pl.BlockSpec(memory_space=pltpu.VMEM)
+    inputs = [pltpu.with_memory_space_constraint(x, pltpu.HBM) for x in (grad_partials, momentum, params, kept)]
     sem = pltpu.SemaphoreType.DMA
-    return pl.pallas_call(
+    results = pl.pallas_call(
         functools.partial(kernel, n_dp, n_fsdp, batches),
-        out_shape=(
-            jax.ShapeDtypeStruct(params.shape, F32),
-            jax.ShapeDtypeStruct(momentum.shape, F32),
-        ),
-        in_specs=[anywhere, anywhere, anywhere, pl.BlockSpec(memory_space=pltpu.SMEM)],
-        out_specs=(anywhere, anywhere),
+        out_shape=(pltpu.VMEM(held, F32), pltpu.VMEM(held, F32)),
+        in_specs=[anywhere, anywhere, anywhere, anywhere],
+        out_specs=(vmem, vmem),
         scratch_shapes=[
+            pltpu.SMEM((KEEP,), jnp.int32),
             pltpu.VMEM((layers, rows, cols), BF16),
             pltpu.VMEM(held, F32),
             pltpu.VMEM(held, F32),
@@ -269,19 +277,28 @@
             pltpu.VMEM((GROUP, 256), BF16),
             pltpu.VMEM((GROUP, 2 * GROUP), BF16),
             pltpu.VMEM((256, PIECE), BF16),
-            pltpu.VMEM(held, F32),
-            pltpu.VMEM(held, F32),
-            sem((3,)),
-            sem((2,)),
+            sem((4,)),
             sem((2, n_fsdp, pieces)),
             sem((2, n_fsdp, pieces)),
             sem((n_dp, len(batches))),
             sem((n_dp, len(batches))),
         ],
         compiler_params=pltpu.CompilerParams(
-            collective_id=0, has_side_effects=True, vmem_limit_bytes=60 * 1024 * 1024
+            collective_id=0, has_side_effects=True, vmem_limit_bytes=48 * 1024 * 1024
         ),
-    )(grad_partials, momentum, params, kept)
+    )(*inputs)
+    results = [pltpu.with_memory_space_constraint(x, pltpu.VMEM) for x in results]
+    return pl.pallas_call(
+        store,
+        out_shape=(
+            jax.ShapeDtypeStruct(params.shape, F32),
+            jax.ShapeDtypeStruct(momentum.shape, F32),
+        ),
+        in_specs=[vmem, vmem],
+        out_specs=(anywhere, anywhere),
+        scratch_shapes=[sem((2,))],
+        compiler_params=pltpu.CompilerParams(vmem_limit_bytes=60 * 1024 * 1024),
+    )(*results)
 
 
 def solution(mesh):

time: 26.6 us -> 23.8 us (0.89)
  local copies, waits for them, and re-layouts: 2.3 us -> 0 us
  Pallas kernels: 23.3 us -> 22.8 us
    unnamed x4 -> x0, local copies, waits for them, and re-layouts: 2.3 us -> none
    pallas_call x1, Pallas kernels: 23.3 us -> 22 us  [shards(): pl.pallas_call(functools.partial(kernel, n_dp, n_fsdp, batches), out_shap...]
    pallas_call x0 -> x1, Pallas kernels: none -> 0.74 us  [shards(): pl.pallas_call(store, out_shape=(jax.ShapeDtypeStruct(params.shape, F32),...]
where the time goes in v2:
time: 23.8 us; the launch traced here: 23.4 us
  Pallas kernels  22.8 us (96%)
  between operations  0.64 us (3%)
    pallas_call x1, Pallas kernels, shards(): pl.pallas_call(functools.partial(kernel, n_dp, n_fsdp, batches), out_shap...  22 us
    pallas_call x1, Pallas kernels, shards(): pl.pallas_call(store, out_shape=(jax.ShapeDtypeStruct(params.shape, F32),...  0.74 us

profile of v2, /device:TPU:0, one launch (start us, length us, event | category | flops | bytes accessed | tf_op | source)
XLA Modules:
  0.0 23.4 jit_solution(383027586261433065)
XLA Ops:
  0.6 22.0 %shard_map.59 = (f32[2,4,5120]{2,1,0:T(4,128)S(1)}, f32[2,4,5120]{2,1,0:T(4,128)S(1)}) custom-call(bf16[1,1,2,16,5120]{4,3,2,1,0:T(8,128)(2,1)} %grad_hbm.1, f32[1,2,4,5120]{3,2,1,0:T(4,128)} %mom_hbm.1, f32[2,4,5120]{2,1,0:T(4,128)} %par_hbm.1, s32[8]{0:T(128)} %kept_hbm.1), custom_call_target="tpu_custom_call" | custom-call | tf_op jit(solution)/shard_map/pallas_call | solution.py:264
  22.7 0.7 %shard_map.60 = (f32[2,4,5120]{2,1,0:T(4,128)}, f32[1,2,4,5120]{3,2,1,0:T(4,128)}) custom-call(f32[2,4,5120]{2,1,0:T(4,128)S(1)} %get-tuple-element.4.new_par, f32[2,4,5120]{2,1,0:T(4,128)S(1)} %get-tuple-element.5.new_mom), custom_call_target="tpu_custom_call" | custom-call | tf_op jit(solution)/shard_map/pallas_call | solution.py:291

commit v3 on v2

v3 whole, which is shorter than its diff:
```python
import functools
import math

import jax
import jax.numpy as jnp
from jax import lax
from jax.experimental import pallas as pl
from jax.experimental.pallas import tpu as pltpu
from jax.sharding import PartitionSpec as P

SPAN = 64
KEEP = 8
PIECE = 1024
GROUP = 256
BURST = 5
WINDOW = 3
SUM_DP, SUM_FSDP = 4, 8
LAG = 2
F32 = jnp.float32
BF16 = jnp.bfloat16


def cosine_rows(k, n):
    turn = ((2 * n + 1) * k) & (4 * SPAN - 1)
    turn = jnp.minimum(turn, 4 * SPAN - turn)
    scale = jnp.where(k == 0, math.sqrt(1.0 / SPAN), math.sqrt(2.0 / SPAN)).astype(F32)
    return scale * jnp.cos(turn.astype(F32) * (math.pi / (2 * SPAN)))


def halves(x):
    high = x.astype(BF16)
    return high, (x - high.astype(F32)).astype(BF16)


def dot(a, b):
    return jnp.dot(a, b, preferred_element_type=F32)


def kernel(
    n_dp, n_fsdp,
    grad_hbm, mom_hbm, par_hbm, kept_hbm, new_par, new_mom,
    kept_ref, grad, mom, par, mine, inbox, own_coef, dp_parts, dp_sum, fsdp_parts, total, w_coef, w_proj, w_back,
    load_sem, send_sem, recv_sem, first_send, first_recv, second_send, second_recv, third_send, third_recv,
):
    layers, rows, cols = grad.shape
    own = rows // n_fsdp
    pieces = cols // PIECE
    parts = PIECE // GROUP
    lanes = 128
    dp, me = lax.axis_index("dp"), lax.axis_index("fsdp")
    mesh_id = pl.DeviceIdType.MESH

    loads = [
        pltpu.make_async_copy(kept_hbm, kept_ref, load_sem.at[0]),
        pltpu.make_async_copy(grad_hbm.at[0, 0], grad, load_sem.at[1]),
        pltpu.make_async_copy(mom_hbm.at[0], mom, load_sem.at[2]),
        pltpu.make_async_copy(par_hbm, par, load_sem.at[3]),
    ]
    for load in loads:
        load.start()

    barrier = pltpu.get_barrier_semaphore()
    for i in range(1, n_fsdp):
        pl.semaphore_signal(barrier, inc=1, device_id={"fsdp": lax.rem(me + i, n_fsdp)}, device_id_type=mesh_id)
    for i in range(1, n_dp):
        pl.semaphore_signal(barrier, inc=1, device_id={"dp": lax.rem(dp + i, n_dp)}, device_id_type=mesh_id)

    near = me // (n_fsdp // 2)
    far = 1 - near
    near_pos = near * (n_fsdp - 1 - me) + far * me
    far_pos = n_fsdp - 1 - near_pos

    loads[0].wait()

    def by_index(shape, dim):
        j = lax.broadcasted_iota(jnp.int32, shape, dim) % KEEP
        k = jnp.zeros(shape, jnp.int32)
        for i in range(KEEP):
            k = jnp.where(j == i, kept_ref[i], k)
        return k

    row = cosine_rows(by_index((KEEP, lanes), 0), lax.broadcasted_iota(jnp.int32, (KEEP, lanes), 1) % SPAN)
    column = cosine_rows(by_index((SPAN, lanes), 1), lax.broadcasted_iota(jnp.int32, (SPAN, lanes), 0))
    lane_block = lax.broadcasted_iota(jnp.int32, (SPAN, lanes), 1) // KEEP
    coef = jnp.concatenate([jnp.where(lane_block == b, column, 0.0) for b in range(GROUP // SPAN)], axis=0)
    wide = jnp.concatenate([row] * (PIECE // lanes), axis=1)
    wide_block = lax.broadcasted_iota(jnp.int32, (KEEP, PIECE), 1) // SPAN
    back = jnp.concatenate([jnp.where(wide_block == b, wide, 0.0) for b in range(PIECE // SPAN)], axis=0)
    high, low = halves(coef)
    w_coef[:, :lanes] = high
    w_coef[:, lanes:] = low
    high, low = halves(back)
    w_back[:lanes] = high
    w_back[lanes:] = low

    loads[1].wait()
    for layer in range(layers):
        for p in range(pieces):
            at = pl.ds(p * PIECE, PIECE)
            x = grad[layer, :, at].astype(F32)
            for d in range(n_fsdp):
                mine[d, layer * own:(layer + 1) * own, at] = x[d * own:(d + 1) * own]

    pl.semaphore_wait(barrier, n_dp - 1 + n_fsdp - 1)

    def forward(flow, q, p):
        at = pl.ds(p * PIECE, PIECE)
        d = flow * (n_fsdp - 1 - q) + (1 - flow) * q
        return pltpu.make_async_remote_copy(
            src_ref=mine.at[d, :, at], dst_ref=inbox.at[flow, d, :, at],
            send_sem=send_sem.at[flow, q, p], recv_sem=recv_sem.at[flow, q, p],
            device_id={"fsdp": me + 1 - 2 * flow}, device_id_type=mesh_id,
        )

    def add(flow, q, p):
        at = pl.ds(p * PIECE, PIECE)
        d = flow * (n_fsdp - 1 - q) + (1 - flow) * q
        forward(flow, q, p).wait_recv()
        mine[d, :, at] += inbox[flow, d, :, at]

    near_list = [(q, p) for q in range(n_fsdp - 1, 0, -1) for p in range(pieces)]
    far_list = [(q, p) for q in range(n_fsdp - 1, n_fsdp // 2, -1) for p in range(pieces)]
    burst = min(BURST, len(near_list))

    @pl.when(near_pos == 0)
    def _():
        for q, p in near_list[:burst]:
            forward(near, q, p).start()

    def first_copy(p):
        return pltpu.make_async_remote_copy(
            src_ref=own_coef.at[p], dst_ref=dp_parts.at[dp],
            send_sem=first_send.at[p], recv_sem=first_recv.at[dp],
            device_id={"dp": p}, device_id_type=mesh_id,
        )

    def first_arrival(source):
        return pltpu.make_async_remote_copy(
            src_ref=own_coef.at[0], dst_ref=dp_parts.at[source],
            send_sem=first_send.at[0], recv_sem=first_recv.at[source],
            device_id={"dp": source}, device_id_type=mesh_id,
        )

    def second_copy(i):
        target = lax.rem(me + i, n_fsdp)
        return pltpu.make_async_remote_copy(
            src_ref=dp_sum.at[target], dst_ref=fsdp_parts.at[me],
            send_sem=second_send.at[i], recv_sem=second_recv.at[me],
            device_id={"fsdp": target}, device_id_type=mesh_id,
        )

    def second_arrival(source):
        return pltpu.make_async_remote_copy(
            src_ref=dp_sum.at[0], dst_ref=fsdp_parts.at[source],
            send_sem=second_send.at[0], recv_sem=second_recv.at[source],
            device_id={"fsdp": source}, device_id_type=mesh_id,
        )

    def third_copy(i):
        return pltpu.make_async_remote_copy(
            src_ref=total.at[dp], dst_ref=total.at[dp],
            send_sem=third_send.at[i], recv_sem=third_recv.at[dp],
            device_id={"dp": lax.rem(dp + i, n_dp)}, device_id_type=mesh_id,
        )

    def third_arrival(p):
        return pltpu.make_async_remote_copy(
            src_ref=total.at[p], dst_ref=total.at[p],
            send_sem=third_send.at[0], recv_sem=third_recv.at[p],
            device_id={"dp": p}, device_id_type=mesh_id,
        )

    def pack(out, height):
        packed = out[:height]
        for q in range(1, parts):
            packed += pltpu.roll(out[q * height:(q + 1) * height], q * (lanes // parts), 1)
        return packed

    def state(p):
        at = pl.ds(p * PIECE, PIECE)
        return 0.9 * jnp.concatenate([mom[layer, :, at] for layer in range(layers)], axis=0)

    def stacked(x):
        return jnp.concatenate([x[:, q * GROUP:(q + 1) * GROUP] for q in range(parts)], axis=0)

    loads[2].wait()
    for p in range(pieces):
        tall = [stacked(grad[layer, :, pl.ds(p * PIECE, PIECE)]) for layer in range(layers)]
        tall += list(halves(stacked(state(p))))
        out = dot(jnp.concatenate(tall, axis=0), w_coef[...])
        out = out[:, :lanes] + out[:, lanes:]
        step = parts * rows
        for layer in range(layers):
            packed = pack(out[layer * step:(layer + 1) * step], rows)
            for d in range(n_fsdp):
                own_coef[p, d, layer * own:(layer + 1) * own] = packed[d * own:(d + 1) * own]
        out = out[layers * step:]
        height = layers * own
        own_coef[p, me] += pack(out[:parts * height] + out[parts * height:], height)

        @pl.when(dp != p)
        def _():
            first_copy(p).start()

    proj = jnp.dot(coef, back[:, :GROUP], precision=lax.Precision.HIGHEST, preferred_element_type=F32)
    high, low = halves(proj)
    w_proj[:, :GROUP] = high
    w_proj[:, GROUP:] = low

    def sum_dp():
        @pl.when(dp < pieces)
        def _():
            dp_parts[dp] = own_coef[dp]
            for i in range(1, n_dp):
                first_arrival(lax.rem(dp + i, n_dp)).wait_recv()
            for d in range(n_fsdp):
                value = dp_parts[0, d]
                for r in range(1, n_dp):
                    value += dp_parts[r, d]
                dp_sum[d] = value
            for i in range(1, n_fsdp):
                second_copy(i).start()

    def sum_fsdp():
        @pl.when(dp < pieces)
        def _():
            fsdp_parts[me] = dp_sum[me]
            for i in range(1, n_fsdp):
                second_arrival(lax.rem(me + i, n_fsdp)).wait_recv()
            value = fsdp_parts[0]
            for f in range(1, n_fsdp):
                value += fsdp_parts[f]
            total[dp] = value
            for i in range(1, n_dp):
                third_copy(i).start()

    def update_params():
        for p in range(pieces):
            @pl.when(dp != p)
            def _():
                third_arrival(p).wait_recv()
        shared = jnp.concatenate([total[p] for p in range(pieces)], axis=0) / n_dp
        high, low = halves(shared)
        left = jnp.concatenate([high, low], axis=0)
        right = jnp.concatenate([high, jnp.zeros_like(low)], axis=0)
        out = dot(jnp.concatenate([left, right], axis=1), w_back[...])
        half = shared.shape[0]
        update = out[:half] + out[half:]
        height = layers * own
        loads[3].wait()
        for p in range(pieces):
            at = pl.ds(p * PIECE, PIECE)
            for layer in range(layers):
                top = p * height + layer * own
                new_par[layer, :, at] = par[layer, :, at] - update[top:top + own]

    def near_step(i):
        q, p = near_list[i]

        if i >= burst:
            @pl.when(near_pos == 0)
            def _():
                for j in range(max(0, burst - WINDOW) if i > burst else 0, i - WINDOW + 1):
                    if i == burst or j == i - WINDOW:
                        forward(near, *near_list[j]).wait_send()
                forward(near, q, p).start()

        if q > 1:
            @pl.when((near_pos > 0) & (near_pos < q))
            def _():
                add(near, q, p)
                forward(near, q, p).start()

    def far_step(q, p):
        @pl.when(far_pos < q)
        def _():
            add(far, q, p)
            forward(far, q, p).start()

    for i in range(len(near_list)):
        near_step(i)
        if 0 <= i - LAG < len(far_list):
            far_step(*far_list[i - LAG])
        if i == min(SUM_DP, len(near_list) - 1):
            sum_dp()
        if i == min(SUM_FSDP, len(near_list) - 1):
            sum_fsdp()

    def finish_sends():
        for q, p in near_list:
            @pl.when((near_pos > 0) & (near_pos < q))
            def _():
                forward(near, q, p).wait_send()
        for q, p in far_list:
            @pl.when(far_pos < q)
            def _():
                forward(far, q, p).wait_send()
        for p in range(pieces):
            @pl.when(dp != p)
            def _():
                first_copy(p).wait_send()

        @pl.when(dp < pieces)
        def _():
            for i in range(1, n_fsdp):
                second_copy(i).wait_send()
            for i in range(1, n_dp):
                third_copy(i).wait_send()

    for p in range(pieces):
        if p == pieces - 2:
            update_params()
        if p == pieces - 1:
            finish_sends()
        add(far, far_pos, p)

        @pl.when(near_pos > 0)
        def _():
            add(near, near_pos, p)

        tall = stacked(state(p) + mine[me, :, pl.ds(p * PIECE, PIECE)])
        half = tall.shape[0]
        out = dot(jnp.concatenate(halves(tall), axis=0), w_proj[...])
        rest = tall - (out[:half, :GROUP] + (out[half:, :GROUP] + out[:half, GROUP:]))
        height = half // parts
        for q in range(parts):
            at = pl.ds(p * PIECE + q * GROUP, GROUP)
            for layer in range(layers):
                new_mom[layer, :, at] = rest[q * height + layer * own:q * height + (layer + 1) * own]

    @pl.when(near_pos == 0)
    def _():
        left = len(near_list) - WINDOW if len(near_list) > burst else 0
        for q, p in near_list[left:]:
            forward(near, q, p).wait_send()


def store(new_par, new_mom, new_par_hbm, new_mom_hbm, sem):
    copies = [
        pltpu.make_async_copy(new_par, new_par_hbm, sem.at[0]),
        pltpu.make_async_copy(new_mom, new_mom_hbm.at[0], sem.at[1]),
    ]
    for copy in copies:
        copy.start()
    for copy in copies:
        copy.wait()


def shards(n_dp, n_fsdp, grad_partials, momentum, params, kept):
    _, _, layers, rows, cols = grad_partials.shape
    own = rows // n_fsdp
    pieces = cols // PIECE
    held = (layers, own, cols)
    tile = (layers * own, 128)
    chunk = (n_fsdp, layers * own, cols)
    anywhere = pl.BlockSpec(memory_space=pl.ANY)
    vmem = pl.BlockSpec(memory_space=pltpu.VMEM)
    inputs = [pltpu.with_memory_space_constraint(x, pltpu.HBM) for x in (grad_partials, momentum, params, kept)]
    sem = pltpu.SemaphoreType.DMA
    results = pl.pallas_call(
        functools.partial(kernel, n_dp, n_fsdp),
        out_shape=(pltpu.VMEM(held, F32), pltpu.VMEM(held, F32)),
        in_specs=[anywhere, anywhere, anywhere, anywhere],
        out_specs=(vmem, vmem),
        scratch_shapes=[
            pltpu.SMEM((KEEP,), jnp.int32),
            pltpu.VMEM((layers, rows, cols), BF16),
            pltpu.VMEM(held, F32),
            pltpu.VMEM(held, F32),
            pltpu.VMEM(chunk, F32),
            pltpu.VMEM((2,) + chunk, F32),
            pltpu.VMEM((pieces, n_fsdp) + tile, F32),
            pltpu.VMEM((n_dp, n_fsdp) + tile, F32),
            pltpu.VMEM((n_fsdp,) + tile, F32),
            pltpu.VMEM((n_fsdp,) + tile, F32),
            pltpu.VMEM((pieces,) + tile, F32),
            pltpu.VMEM((GROUP, 256), BF16),
            pltpu.VMEM((GROUP, 2 * GROUP), BF16),
            pltpu.VMEM((256, PIECE), BF16),
            sem((4,)),
            sem((2, n_fsdp, pieces)),
            sem((2, n_fsdp, pieces)),
            sem((pieces,)),
            sem((n_dp,)),
            sem((n_fsdp,)),
            sem((n_fsdp,)),
            sem((n_dp,)),
            sem((pieces,)),
        ],
        compiler_params=pltpu.CompilerParams(
            collective_id=0, has_side_effects=True, vmem_limit_bytes=48 * 1024 * 1024
        ),
    )(*inputs)
    results = [pltpu.with_memory_space_constraint(x, pltpu.VMEM) for x in results]
    return pl.pallas_call(
        store,
        out_shape=(
            jax.ShapeDtypeStruct(params.shape, F32),
            jax.ShapeDtypeStruct(momentum.shape, F32),
        ),
        in_specs=[vmem, vmem],
        out_specs=(anywhere, anywhere),
        scratch_shapes=[sem((2,))],
        compiler_params=pltpu.CompilerParams(vmem_limit_bytes=60 * 1024 * 1024),
    )(*results)


def solution(mesh):
    placed = (
        P("dp", "fsdp", None, None, None),
        P("dp", None, "fsdp", None),
        P(None, "fsdp", None),
        P(),
    )
    return jax.shard_map(
        functools.partial(shards, mesh.shape["dp"], mesh.shape["fsdp"]),
        mesh=mesh,
        in_specs=placed,
        out_specs=(P(None, "fsdp", None), P("dp", None, "fsdp", None)),
        check_vma=False,
    )
```

time: 23.8 us -> 23.4 us (0.983)
  the two profiles are of different devices: /device:TPU:0 before, /device:TPU:8 now
where the time goes in v3:
time: 23.4 us; the launch traced here: 23.2 us
  Pallas kernels  22.6 us (97%)
  between operations  0.64 us (3%)
    pallas_call x1, Pallas kernels, shards(): pl.pallas_call(functools.partial(kernel, n_dp, n_fsdp), out_shape=(pltpu....  21.9 us
    pallas_call x1, Pallas kernels, shards(): pl.pallas_call(store, out_shape=(jax.ShapeDtypeStruct(params.shape, F32),...  0.74 us

profile of v3, /device:TPU:8, one launch (start us, length us, event | category | flops | bytes accessed | tf_op | source)
XLA Modules:
  0.0 23.2 jit_solution(6253624749217944045)
XLA Ops:
  0.6 21.9 %shard_map.59 = (f32[2,4,5120]{2,1,0:T(4,128)S(1)}, f32[2,4,5120]{2,1,0:T(4,128)S(1)}) custom-call(bf16[1,1,2,16,5120]{4,3,2,1,0:T(8,128)(2,1)} %grad_hbm.1, f32[1,2,4,5120]{3,2,1,0:T(4,128)} %mom_hbm.1, f32[2,4,5120]{2,1,0:T(4,128)} %par_hbm.1, s32[8]{0:T(128)} %kept_hbm.1), custom_call_target="tpu_custom_call" | custom-call | tf_op jit(solution)/shard_map/pallas_call | solution.py:360
  22.5 0.7 %shard_map.60 = (f32[2,4,5120]{2,1,0:T(4,128)}, f32[1,2,4,5120]{3,2,1,0:T(4,128)}) custom-call(f32[2,4,5120]{2,1,0:T(4,128)S(1)} %get-tuple-element.4.new_par, f32[2,4,5120]{2,1,0:T(4,128)S(1)} %get-tuple-element.5.new_mom), custom_call_target="tpu_custom_call" | custom-call | tf_op jit(solution)/shard_map/pallas_call | solution.py:395

commit v4 on v3

--- a/solution.py
+++ b/solution.py
@@ -12,9 +12,8 @@
 KEEP = 8
 PIECE = 1024
 GROUP = 256
-BURST = 5
-WINDOW = 3
-SUM_DP, SUM_FSDP = 4, 8
+BURST = 7
+SUM_DP, SUM_FSDP = 2, 8
 LAG = 2
 F32 = jnp.float32
 BF16 = jnp.bfloat16
@@ -70,6 +69,40 @@
     near_pos = near * (n_fsdp - 1 - me) + far * me
     far_pos = n_fsdp - 1 - near_pos
 
+    loads[1].wait()
+    for layer in range(layers):
+        for p in range(pieces):
+            at = pl.ds(p * PIECE, PIECE)
+            x = grad[layer, :, at].astype(F32)
+            for d in range(n_fsdp):
+                mine[d, layer * own:(layer + 1) * own, at] = x[d * own:(d + 1) * own]
+
+    pl.semaphore_wait(barrier, n_dp - 1 + n_fsdp - 1)
+
+    def forward(flow, q, p):
+        at = pl.ds(p * PIECE, PIECE)
+        d = flow * (n_fsdp - 1 - q) + (1 - flow) * q
+        return pltpu.make_async_remote_copy(
+            src_ref=mine.at[d, :, at], dst_ref=inbox.at[flow, d, :, at],
+            send_sem=send_sem.at[flow, q, p], recv_sem=recv_sem.at[flow, q, p],
+            device_id={"fsdp": me + 1 - 2 * flow}, device_id_type=mesh_id,
+        )
+
+    def add(flow, q, p):
+        at = pl.ds(p * PIECE, PIECE)
+        d = flow * (n_fsdp - 1 - q) + (1 - flow) * q
+        forward(flow, q, p).wait_recv()
+        mine[d, :, at] += inbox[flow, d, :, at]
+
+    near_list = [(q, p) for q in range(n_fsdp - 1, 0, -1) for p in range(pieces)]
+    far_list = [(q, p) for q in range(n_fsdp - 1, n_fsdp // 2, -1) for p in range(pieces)]
+    burst = min(BURST, len(near_list))
+
+    @pl.when(near_pos == 0)
+    def _():
+        for q, p in near_list[:burst]:
+            forward(near, q, p).start()
+
     loads[0].wait()
 
     def by_index(shape, dim):
@@ -92,40 +125,6 @@
     high, low = halves(back)
     w_back[:lanes] = high
     w_back[lanes:] = low
-
-    loads[1].wait()
-    for layer in range(layers):
-        for p in range(pieces):
-            at = pl.ds(p * PIECE, PIECE)
-            x = grad[layer, :, at].astype(F32)
-            for d in range(n_fsdp):
-                mine[d, layer * own:(layer + 1) * own, at] = x[d * own:(d + 1) * own]
-
-    pl.semaphore_wait(barrier, n_dp - 1 + n_fsdp - 1)
-
-    def forward(flow, q, p):
-        at = pl.ds(p * PIECE, PIECE)
-        d = flow * (n_fsdp - 1 - q) + (1 - flow) * q
-        return pltpu.make_async_remote_copy(
-            src_ref=mine.at[d, :, at], dst_ref=inbox.at[flow, d, :, at],
-            send_sem=send_sem.at[flow, q, p], recv_sem=recv_sem.at[flow, q, p],
-            device_id={"fsdp": me + 1 - 2 * flow}, device_id_type=mesh_id,
-        )
-
-    def add(flow, q, p):
-        at = pl.ds(p * PIECE, PIECE)
-        d = flow * (n_fsdp - 1 - q) + (1 - flow) * q
-        forward(flow, q, p).wait_recv()
-        mine[d, :, at] += inbox[flow, d, :, at]
-
-    near_list = [(q, p) for q in range(n_fsdp - 1, 0, -1) for p in range(pieces)]
-    far_list = [(q, p) for q in range(n_fsdp - 1, n_fsdp // 2, -1) for p in range(pieces)]
-    burst = min(BURST, len(near_list))
-
-    @pl.when(near_pos == 0)
-    def _():
-        for q, p in near_list[:burst]:
-            forward(near, q, p).start()
 
     def first_copy(p):
         return pltpu.make_async_remote_copy(
@@ -257,14 +256,6 @@
     def near_step(i):
         q, p = near_list[i]
 
-        if i >= burst:
-            @pl.when(near_pos == 0)
-            def _():
-                for j in range(max(0, burst - WINDOW) if i > burst else 0, i - WINDOW + 1):
-                    if i == burst or j == i - WINDOW:
-                        forward(near, *near_list[j]).wait_send()
-                forward(near, q, p).start()
-
         if q > 1:
             @pl.when((near_pos > 0) & (near_pos < q))
             def _():
@@ -277,14 +268,21 @@
             add(far, q, p)
             forward(far, q, p).start()
 
+    @pl.when(near_pos == 0)
+    def _():
+        sum_dp()
+        for q, p in near_list[burst:]:
+            forward(near, q, p).start()
+        sum_fsdp()
+
     for i in range(len(near_list)):
         near_step(i)
         if 0 <= i - LAG < len(far_list):
             far_step(*far_list[i - LAG])
         if i == min(SUM_DP, len(near_list) - 1):
-            sum_dp()
+            pl.when(near_pos > 0)(sum_dp)
         if i == min(SUM_FSDP, len(near_list) - 1):
-            sum_fsdp()
+            pl.when(near_pos > 0)(sum_fsdp)
 
     def finish_sends():
         for q, p in near_list:
@@ -330,8 +328,7 @@
 
     @pl.when(near_pos == 0)
     def _():
-        left = len(near_list) - WINDOW if len(near_list) > burst else 0
-        for q, p in near_list[left:]:
+        for q, p in near_list:
             forward(near, q, p).wait_send()
 
 

time: 23.4 us -> 21 us (0.90)
  the two profiles are of different devices: /device:TPU:8 before, /device:TPU:0 now
where the time goes in v4:
time: 21 us; the launch traced here: 20.9 us
  Pallas kernels  20.2 us (96%)
  between operations  0.64 us (3%)
    pallas_call x1, Pallas kernels, shards(): pl.pallas_call(functools.partial(kernel, n_dp, n_fsdp), out_shape=(pltpu....  19.5 us
    pallas_call x1, Pallas kernels, shards(): pl.pallas_call(store, out_shape=(jax.ShapeDtypeStruct(params.shape, F32),...  0.74 us

profile of v4, /device:TPU:0, one launch (start us, length us, event | category | flops | bytes accessed | tf_op | source)
XLA Modules:
  0.0 20.9 jit_solution(4810379198550286252)
XLA Ops:
  0.6 19.5 %shard_map.59 = (f32[2,4,5120]{2,1,0:T(4,128)S(1)}, f32[2,4,5120]{2,1,0:T(4,128)S(1)}) custom-call(bf16[1,1,2,16,5120]{4,3,2,1,0:T(8,128)(2,1)} %grad_hbm.1, f32[1,2,4,5120]{3,2,1,0:T(4,128)} %mom_hbm.1, f32[2,4,5120]{2,1,0:T(4,128)} %par_hbm.1, s32[8]{0:T(128)} %kept_hbm.1), custom_call_target="tpu_custom_call" | custom-call | tf_op jit(solution)/shard_map/pallas_call | solution.py:357
  20.1 0.7 %shard_map.60 = (f32[2,4,5120]{2,1,0:T(4,128)}, f32[1,2,4,5120]{3,2,1,0:T(4,128)}) custom-call(f32[2,4,5120]{2,1,0:T(4,128)S(1)} %get-tuple-element.4.new_par, f32[2,4,5120]{2,1,0:T(4,128)S(1)} %get-tuple-element.5.new_mom), custom_call_target="tpu_custom_call" | custom-call | tf_op jit(solution)/shard_map/pallas_call | solution.py:392

commit v5 on v4

--- a/solution.py
+++ b/solution.py
@@ -12,8 +12,8 @@
 KEEP = 8
 PIECE = 1024
 GROUP = 256
-BURST = 7
-SUM_DP, SUM_FSDP = 2, 8
+BURST = 6
+SUM_DP, SUM_FSDP = 2, 7
 LAG = 2
 F32 = jnp.float32
 BF16 = jnp.bfloat16
@@ -305,26 +305,30 @@
             for i in range(1, n_dp):
                 third_copy(i).wait_send()
 
-    for p in range(pieces):
-        if p == pieces - 2:
+    height = layers * own
+    groups = [range(p, min(p + 2, pieces)) for p in range(0, pieces, 2)]
+    for g, group in enumerate(groups):
+        if g == min(1, len(groups) - 1):
             update_params()
-        if p == pieces - 1:
+        if g == len(groups) - 1:
             finish_sends()
-        add(far, far_pos, p)
-
-        @pl.when(near_pos > 0)
-        def _():
-            add(near, near_pos, p)
-
-        tall = stacked(state(p) + mine[me, :, pl.ds(p * PIECE, PIECE)])
+        tall = []
+        for p in group:
+            add(far, far_pos, p)
+
+            @pl.when(near_pos > 0)
+            def _():
+                add(near, near_pos, p)
+
+            tall.append(stacked(state(p) + mine[me, :, pl.ds(p * PIECE, PIECE)]))
+        tall = jnp.concatenate(tall, axis=0)
         half = tall.shape[0]
         out = dot(jnp.concatenate(halves(tall), axis=0), w_proj[...])
         rest = tall - (out[:half, :GROUP] + (out[half:, :GROUP] + out[:half, GROUP:]))
-        height = half // parts
-        for q in range(parts):
-            at = pl.ds(p * PIECE + q * GROUP, GROUP)
+        for j in range(len(group) * parts):
+            at = pl.ds(group[0] * PIECE + j * GROUP, GROUP)
             for layer in range(layers):
-                new_mom[layer, :, at] = rest[q * height + layer * own:q * height + (layer + 1) * own]
+                new_mom[layer, :, at] = rest[j * height + layer * own:j * height + (layer + 1) * own]
 
     @pl.when(near_pos == 0)
     def _():

time: 21 us -> 21 us (level)
  no operation moved by 1% of the time
where the time goes in v5:
time: 21 us; the launch traced here: 20.9 us
  Pallas kernels  20.3 us (97%)
  between operations  0.64 us (3%)
    pallas_call x1, Pallas kernels, shards(): pl.pallas_call(functools.partial(kernel, n_dp, n_fsdp), out_shape=(pltpu....  19.5 us
    pallas_call x1, Pallas kernels, shards(): pl.pallas_call(store, out_shape=(jax.ShapeDtypeStruct(params.shape, F32),...  0.74 us

profile of v5, /device:TPU:0, one launch (start us, length us, event | category | flops | bytes accessed | tf_op | source)
XLA Modules:
  0.0 20.9 jit_solution(14257592774337776508)
XLA Ops:
  0.6 19.5 %shard_map.59 = (f32[2,4,5120]{2,1,0:T(4,128)S(1)}, f32[2,4,5120]{2,1,0:T(4,128)S(1)}) custom-call(bf16[1,1,2,16,5120]{4,3,2,1,0:T(8,128)(2,1)} %grad_hbm.1, f32[1,2,4,5120]{3,2,1,0:T(4,128)} %mom_hbm.1, f32[2,4,5120]{2,1,0:T(4,128)} %par_hbm.1, s32[8]{0:T(128)} %kept_hbm.1), custom_call_target="tpu_custom_call" | custom-call | tf_op jit(solution)/shard_map/pallas_call | solution.py:361
  20.2 0.7 %shard_map.60 = (f32[2,4,5120]{2,1,0:T(4,128)}, f32[1,2,4,5120]{3,2,1,0:T(4,128)}) custom-call(f32[2,4,5120]{2,1,0:T(4,128)S(1)} %get-tuple-element.4.new_par, f32[2,4,5120]{2,1,0:T(4,128)S(1)} %get-tuple-element.5.new_mom), custom_call_target="tpu_custom_call" | custom-call | tf_op jit(solution)/shard_map/pallas_call | solution.py:396

commit v6 on v5

--- a/solution.py
+++ b/solution.py
@@ -69,16 +69,6 @@
     near_pos = near * (n_fsdp - 1 - me) + far * me
     far_pos = n_fsdp - 1 - near_pos
 
-    loads[1].wait()
-    for layer in range(layers):
-        for p in range(pieces):
-            at = pl.ds(p * PIECE, PIECE)
-            x = grad[layer, :, at].astype(F32)
-            for d in range(n_fsdp):
-                mine[d, layer * own:(layer + 1) * own, at] = x[d * own:(d + 1) * own]
-
-    pl.semaphore_wait(barrier, n_dp - 1 + n_fsdp - 1)
-
     def forward(flow, q, p):
         at = pl.ds(p * PIECE, PIECE)
         d = flow * (n_fsdp - 1 - q) + (1 - flow) * q
@@ -96,11 +86,24 @@
 
     near_list = [(q, p) for q in range(n_fsdp - 1, 0, -1) for p in range(pieces)]
     far_list = [(q, p) for q in range(n_fsdp - 1, n_fsdp // 2, -1) for p in range(pieces)]
-    burst = min(BURST, len(near_list))
+    burst = max(pieces, min(BURST, len(near_list)))
+
+    loads[1].wait()
+    pl.semaphore_wait(barrier, n_dp - 1 + n_fsdp - 1)
+    for p in range(pieces):
+        at = pl.ds(p * PIECE, PIECE)
+        for layer in range(layers):
+            x = grad[layer, :, at].astype(F32)
+            for d in range(n_fsdp):
+                mine[d, layer * own:(layer + 1) * own, at] = x[d * own:(d + 1) * own]
+
+        @pl.when(near_pos == 0)
+        def _():
+            forward(near, *near_list[p]).start()
 
     @pl.when(near_pos == 0)
     def _():
-        for q, p in near_list[:burst]:
+        for q, p in near_list[pieces:burst]:
             forward(near, q, p).start()
 
     loads[0].wait()

time: 21 us -> 21.1 us (level)
  no operation moved by 1% of the time
where the time goes in v6:
time: 21.1 us; the launch traced here: 20.9 us
  Pallas kernels  20.3 us (96%)
  between operations  0.64 us (3%)
    pallas_call x1, Pallas kernels, shards(): pl.pallas_call(functools.partial(kernel, n_dp, n_fsdp), out_shape=(pltpu....  19.5 us
    pallas_call x1, Pallas kernels, shards(): pl.pallas_call(store, out_shape=(jax.ShapeDtypeStruct(params.shape, F32),...  0.74 us

profile of v6, /device:TPU:0, one launch (start us, length us, event | category | flops | bytes accessed | tf_op | source)
XLA Modules:
  0.0 20.9 jit_solution(5494463126282446282)
XLA Ops:
  0.6 19.5 %shard_map.59 = (f32[2,4,5120]{2,1,0:T(4,128)S(1)}, f32[2,4,5120]{2,1,0:T(4,128)S(1)}) custom-call(bf16[1,1,2,16,5120]{4,3,2,1,0:T(8,128)(2,1)} %grad_hbm.1, f32[1,2,4,5120]{3,2,1,0:T(4,128)} %mom_hbm.1, f32[2,4,5120]{2,1,0:T(4,128)} %par_hbm.1, s32[8]{0:T(128)} %kept_hbm.1), custom_call_target="tpu_custom_call" | custom-call | tf_op jit(solution)/shard_map/pallas_call | solution.py:364
  20.2 0.7 %shard_map.60 = (f32[2,4,5120]{2,1,0:T(4,128)}, f32[1,2,4,5120]{3,2,1,0:T(4,128)}) custom-call(f32[2,4,5120]{2,1,0:T(4,128)S(1)} %get-tuple-element.4.new_par, f32[2,4,5120]{2,1,0:T(4,128)S(1)} %get-tuple-element.5.new_mom), custom_call_target="tpu_custom_call" | custom-call | tf_op jit(solution)/shard_map/pallas_call | solution.py:399
